TPU v7x, 512 devices: a whole 4x8x8 slice. The times are simulated.
512 devices in a mesh: blk: 128 (over x, y_hi, z, core), pair: 4 (over y_lo).
Axes of the slice: x: 4, y: 8 (y_hi: 2, y_lo: 4; y = y_hi * 4 + y_lo), z: 8, core: 2. Of those that a mesh axis runs over, the one named last changes fastest.
Arguments:
- half_blocks: bfloat16 [16384, 32, 256], P('blk', 'pair'), may hold values from -6 to 6
- row_target: int32 [16384], P('blk'), may hold values from 0 to 16383, as said below
- vir_coeff: bfloat16 [256, 128], replicated, may hold values from -0.375 to 0.375
- occ_energy: float32 [32], replicated, may hold values from -2 to -0.3
- vir_energy: float32 [128], replicated, may hold values from 0.1 to 3
- freq_pick: int32 [6], replicated, may hold values from 0 to 31
Outputs:
- response: float32 [6, 16384, 1024], P(None, 'blk', 'pair')
Inputs may be any that keep to these rules, and one draw needn't show every extreme that they name: row_target is a permutation of the auxiliary functions. The rows of one device go at most 2 to the block of 128 functions of any one owner; every device sends exactly 2 rows to some owner, and every owner receives exactly 2 rows from some device. All devices send the same counts of rows, to owners paired in different ways.
All inputs are finite; a program needn't handle non-finite values.
Results may differ from a plain program's by a relative error of at most 0.0024.
Values may be sent and summed in bfloat16 or wider, within the bound.
A program may use at most 64 MiB of HBM per device.

v0:
```python
import math

import jax
import jax.numpy as jnp
from jax import lax
from jax.sharding import PartitionSpec as P

STOPS = 8
GRID = 32


def from_behind(x, axis, by):
    devices = lax.axis_size(axis)
    return lax.ppermute(x, axis, [(i, (i + by) % devices) for i in range(devices)])


def response_factor(occ_values, vir_values, frequency):
    energy_gap = vir_values[None, :] - occ_values[:, None]
    factor = (
        2.0
        * energy_gap[None]
        / (
            energy_gap[None] * energy_gap[None]
            + frequency[:, None, None] * frequency[:, None, None]
        )
    )
    return factor.reshape(frequency.shape[0], -1)


def to_virtual(blocks, coeff):
    row_count, occ_count, basis = blocks.shape
    product = jnp.dot(
        blocks.reshape(row_count * occ_count, basis), coeff, preferred_element_type=jnp.float32
    )
    return product.astype(jnp.bfloat16).reshape(row_count, occ_count * coeff.shape[1])


def put_rows(arrived, arrived_ids, row_count):
    safe_ids = jnp.where(arrived_ids >= 0, arrived_ids, row_count)
    empty = jnp.zeros((row_count, arrived.shape[1]), arrived.dtype)
    return empty.at[safe_ids].set(arrived, mode="drop")


def shards(half_blocks, row_target, vir_coeff, occ_energy, vir_energy, freq_pick):
    blk_count = lax.axis_size("blk")
    row_count, occ_dev, basis = half_blocks.shape
    virtual = vir_coeff.shape[1]
    capacity = min(row_count, 2 * max(1, row_count // blk_count))
    owners = row_target // row_count
    onehot = (owners[:, None] == jnp.arange(blk_count, dtype=jnp.int32)[None, :]).astype(jnp.int32)
    earlier = jnp.cumsum(onehot, axis=0) - onehot
    position = owners * capacity + jnp.sum(earlier * onehot, axis=1)
    landing = (
        jnp.full((blk_count * capacity,), -1, jnp.int32).at[position].set(row_target % row_count)
    )
    payload = half_blocks.reshape(row_count, occ_dev * basis)
    outgoing = (
        jnp.zeros((blk_count * capacity, payload.shape[1]), jnp.bfloat16).at[position].set(payload)
    )
    arrived, arrived_ids = (
        lax.all_to_all(outgoing, "blk", split_axis=0, concat_axis=0, tiled=True),
        lax.all_to_all(landing, "blk", split_axis=0, concat_axis=0, tiled=True),
    )
    placed = put_rows(arrived, arrived_ids, row_count)
    virt_rows = to_virtual(placed.reshape(row_count, occ_dev, basis), vir_coeff)
    frequency = 0.5 * jnp.tan(jnp.pi * (freq_pick.astype(jnp.float32) + 0.5) / (2.0 * GRID))
    lowest = STOPS // 2 - 1
    scaling = 1.0 / math.sqrt(occ_energy.shape[0] * virtual)
    freq_count = frequency.shape[0]
    current = from_behind(virt_rows, "blk", lowest)
    pieces = [current]
    for stop in range(1, STOPS):
        current = from_behind(current, "blk", -1)
        pieces.append(current)
    own_occ = lax.dynamic_slice_in_dim(occ_energy, lax.axis_index("pair") * occ_dev, occ_dev)
    factor = response_factor(own_occ, vir_energy, frequency)
    weighted = (virt_rows.astype(jnp.float32)[None] * factor[:, None, :]).astype(jnp.bfloat16)
    partners = jnp.concatenate(pieces, axis=0)
    tiles = lax.dot_general(
        weighted.reshape(freq_count * row_count, -1),
        partners,
        (((1,), (1,)), ((), ())),
        preferred_element_type=jnp.float32,
    )
    summed = lax.psum_scatter(
        tiles.reshape(freq_count, row_count, -1), "pair", scatter_dimension=2, tiled=True
    )
    return summed * scaling


def solution(mesh):
    return jax.shard_map(
        shards,
        mesh=mesh,
        in_specs=(P("blk", "pair", None), P("blk"), P(), P(), P(), P()),
        out_specs=P(None, "blk", "pair"),
        check_vma=False,
    )
```

profile of v0, /device:TPU:1, one launch (start us, length us, event | category | flops | bytes accessed | tf_op | source)
XLA Modules:
  0.0 289.7 jit_solution(17630439050682472903)
XLA Ops:
  6.5 0.7 and_select_fusion
  7.7 1.0 scatter_custom_fusion
  8.7 0.8 all_to_all.16
  9.4 20.9 %all-to-all-start = ((s32[128,2,1]{1,2,0:T(1,128)}), s32[128,2,1]{1,2,0:T(1,128)S(1)}, u32[]{:S(2)}, u32[]{:S(2)}) async-start(s32[128,2,1]{1,2,0:T(1,128)} %bitcast), calls=%async_computation | async-start | bytes 131072 | tf_op jit(solution)/shard_map/all_to_all | solution.py:62
  30.3 1.2 copy.8
  31.5 1.7 scatter_custom_fusion.1
  33.2 1.5 all_to_all.19
  34.7 10.1 %all-to-all-done = s32[128,2,1]{1,2,0:T(1,128)S(1)} async-done(((s32[128,2,1]{1,2,0:T(1,128)}), s32[128,2,1]{1,2,0:T(1,128)S(1)}, u32[]{:S(2)}, u32[]{:S(2)}) %all-to-all-start) | async-done | bytes 1056 | tf_op jit(solution)/shard_map/all_to_all | solution.py:62
  44.8 6.1 %all-to-all-start.1 = ((bf16[128,2,2048]{2,1,0:T(2,128)(2,1)}), bf16[128,2,2048]{2,1,0:T(2,128)(2,1)S(1)}, u32[]{:S(2)}, u32[]{:S(2)}) async-start(bf16[128,2,2048]{2,1,0:T(2,128)(2,1)} %all_to_all.19), calls=%async_computation.1 | async-start | bytes 2097152 | tf_op jit(solution)/shard_map/all_to_all | solution.py:61
  51.0 0.5 broadcast.136
  51.5 0.8 reduce.3
  52.5 28.1 %all-to-all-done.1 = bf16[128,2,2048]{2,1,0:T(2,128)(2,1)S(1)} async-done(((bf16[128,2,2048]{2,1,0:T(2,128)(2,1)}), bf16[128,2,2048]{2,1,0:T(2,128)(2,1)S(1)}, u32[]{:S(2)}, u32[]{:S(2)}) %all-to-all-start.1) | async-done | bytes 1048608 | tf_op jit(solution)/shard_map/all_to_all | solution.py:61
  81.0 2.2 scatter_custom_fusion.2
  83.9 3.7 %collective-permute-start = (bf16[128,1024]{1,0:T(8,128)(2,1)S(1)}, bf16[128,1024]{1,0:T(8,128)(2,1)S(1)}, u32[]{:S(2)}, u32[]{:S(2)}) collective-permute-start(bf16[128,1024]{1,0:T(8,128)(2,1)S(1)} %reshape.117), channel_id=1, source_target_pairs={{0,12},{4,16},{8,20},{12,24},{16,28},{20,32},{24,36},{28,40},{32,4... | collective-permute-start | bytes 786440 | tf_op jit(solution)/shard_map/ppermute | solution.py:14
  87.6 16.9 %collective-permute-done = bf16[128,1024]{1,0:T(8,128)(2,1)S(1)} collective-permute-done((bf16[128,1024]{1,0:T(8,128)(2,1)S(1)}, bf16[128,1024]{1,0:T(8,128)(2,1)S(1)}, u32[]{:S(2)}, u32[]{:S(2)}) %collective-permute-start) | collective-permute-done | bytes 262176 | tf_op jit(solution)/shard_map/ppermute | solution.py:14
  104.5 1.9 collective-permute-start.1
  106.4 6.4 %collective-permute-done.1 = bf16[128,1024]{1,0:T(8,128)(2,1)S(1)} collective-permute-done((bf16[128,1024]{1,0:T(8,128)(2,1)S(1)}, bf16[128,1024]{1,0:T(8,128)(2,1)S(1)}, u32[]{:S(2)}, u32[]{:S(2)}) %collective-permute-start.1) | collective-permute-done | bytes 262176 | tf_op jit(solution)/shard_map/ppermute | solution.py:14
  112.7 1.9 collective-permute-start.2
  114.6 5.8 %collective-permute-done.2 = bf16[128,1024]{1,0:T(8,128)(2,1)S(1)} collective-permute-done((bf16[128,1024]{1,0:T(8,128)(2,1)S(1)}, bf16[128,1024]{1,0:T(8,128)(2,1)S(1)}, u32[]{:S(2)}, u32[]{:S(2)}) %collective-permute-start.2) | collective-permute-done | bytes 262176 | tf_op jit(solution)/shard_map/ppermute | solution.py:14
  120.4 6.5 %collective-permute-start.3 = (bf16[128,1024]{1,0:T(8,128)(2,1)S(1)}, bf16[128,1024]{1,0:T(8,128)(2,1)S(1)}, u32[]{:S(2)}, u32[]{:S(2)}) collective-permute-start(bf16[128,1024]{1,0:T(8,128)(2,1)S(1)} %collective-permute-done.2), channel_id=1, source_target_pairs={{0,508},{4,0},{8,4},{12,8},{16,12},{20,16},{24,20},{28,24},{32,28}... | collective-permute-start | bytes 786440 | tf_op jit(solution)/shard_map/ppermute | solution.py:14
  126.9 1.2 collective-permute-done.3
  128.1 14.6 %collective-permute-start.4 = (bf16[128,1024]{1,0:T(8,128)(2,1)S(1)}, bf16[128,1024]{1,0:T(8,128)(2,1)S(1)}, u32[]{:S(2)}, u32[]{:S(2)}) collective-permute-start(bf16[128,1024]{1,0:T(8,128)(2,1)S(1)} %collective-permute-done.3), channel_id=1, source_target_pairs={{0,508},{4,0},{8,4},{12,8},{16,12},{20,16},{24,20},{28,24},{32,28}... | collective-permute-start | bytes 786440 | tf_op jit(solution)/shard_map/ppermute | solution.py:14
  142.9 0.9 collective-permute-done.4
  143.8 17.5 %collective-permute-start.5 = (bf16[128,1024]{1,0:T(8,128)(2,1)S(1)}, bf16[128,1024]{1,0:T(8,128)(2,1)S(1)}, u32[]{:S(2)}, u32[]{:S(2)}) collective-permute-start(bf16[128,1024]{1,0:T(8,128)(2,1)S(1)} %collective-permute-done.4), channel_id=1, source_target_pairs={{0,508},{4,0},{8,4},{12,8},{16,12},{20,16},{24,20},{28,24},{32,28}... | collective-permute-start | bytes 786440 | tf_op jit(solution)/shard_map/ppermute | solution.py:14
  161.5 1.0 collective-permute-done.5
  162.5 16.4 %collective-permute-start.6 = (bf16[128,1024]{1,0:T(8,128)(2,1)S(1)}, bf16[128,1024]{1,0:T(8,128)(2,1)S(1)}, u32[]{:S(2)}, u32[]{:S(2)}) collective-permute-start(bf16[128,1024]{1,0:T(8,128)(2,1)S(1)} %collective-permute-done.5), channel_id=1, source_target_pairs={{0,508},{4,0},{8,4},{12,8},{16,12},{20,16},{24,20},{28,24},{32,28}... | collective-permute-start | bytes 786440 | tf_op jit(solution)/shard_map/ppermute | solution.py:14
  178.9 1.1 collective-permute-done.6
  180.0 14.9 %collective-permute-start.7 = (bf16[128,1024]{1,0:T(8,128)(2,1)S(1)}, bf16[128,1024]{1,0:T(8,128)(2,1)S(1)}, u32[]{:S(2)}, u32[]{:S(2)}) collective-permute-start(bf16[128,1024]{1,0:T(8,128)(2,1)S(1)} %collective-permute-done.6), channel_id=1, source_target_pairs={{0,508},{4,0},{8,4},{12,8},{16,12},{20,16},{24,20},{28,24},{32,28}... | collective-permute-start | bytes 786440 | tf_op jit(solution)/shard_map/ppermute | solution.py:14
  195.0 1.1 collective-permute-done.7
  196.1 3.5 %fusion = f32[6,128,1024]{2,1,0:T(8,128)} fusion(bf16[1024,1024]{1,0:T(8,128)(2,1)S(1)} %constant_dynamic-update-slice_fusion, f32[6,1024]{1,0:T(8,128)S(1)} %add_divide_fusion, f32[128,1024]{1,0:T(8,128)S(1)} %convert_element_type.23), kind=kOutput, calls=%fused_computation.4 | convolution fusion | flops 1612185600 | bytes 5791744 | tf_op jit(solution)/shard_map/dot_general | solution.py:79
  199.6 81.2 %reduce-scatter.2.cloned.1.call-done = f32[6,128,256]{2,1,0:T(8,128)} async-done(((f32[6,128,1024]{2,1,0:T(8,128)}), f32[6,128,256]{2,1,0:T(8,128)}) %reduce-scatter.2.cloned.1.call-update) | async-done | bytes 786448 | tf_op jit(solution)/shard_map/reduce_scatter | solution.py:85
  280.8 2.1 broadcast_multiply_fusion
  (34 shorter events, 2.2 us)
Async XLA Ops:
  6.5 76.9 %copy-start = (bf16[256,128]{1,0:T(8,128)(2,1)S(1)}, bf16[256,128]{1,0:T(8,128)(2,1)}, u32[]{:S(2)}) copy-start(bf16[256,128]{1,0:T(8,128)(2,1)} %param.8) | copy-start | bytes 196612
  9.4 35.4 %all-to-all-start = ((s32[128,2,1]{1,2,0:T(1,128)}), s32[128,2,1]{1,2,0:T(1,128)S(1)}, u32[]{:S(2)}, u32[]{:S(2)}) async-start(s32[128,2,1]{1,2,0:T(1,128)} %bitcast), calls=%async_computation | async-start | bytes 131072 | tf_op jit(solution)/shard_map/all_to_all | solution.py:62
  44.8 35.8 %all-to-all-start.1 = ((bf16[128,2,2048]{2,1,0:T(2,128)(2,1)}), bf16[128,2,2048]{2,1,0:T(2,128)(2,1)S(1)}, u32[]{:S(2)}, u32[]{:S(2)}) async-start(bf16[128,2,2048]{2,1,0:T(2,128)(2,1)} %all_to_all.19), calls=%async_computation.1 | async-start | bytes 2097152 | tf_op jit(solution)/shard_map/all_to_all | solution.py:61
  50.9 229.8 %reduce-scatter.2.cloned.1.call-start = ((), (), s32[]{:S(2)}) async-start(), calls=%async_computation.3 | async-start | bytes 3932160 | tf_op jit(solution)/shard_map/reduce_scatter | solution.py:85
  52.5 90.2 %copy-start.2 = (s32[6]{0:T(128)S(1)}, s32[6]{0:T(128)}, u32[]{:S(2)}) copy-start(s32[6]{0:T(128)} %param.11) | copy-start | bytes 76
  52.5 90.3 %copy-start.3 = (f32[32]{0:T(128)S(1)}, f32[32]{0:T(128)}, u32[]{:S(2)}) copy-start(f32[32]{0:T(128)} %param.9) | copy-start | bytes 388
  52.5 90.4 %copy-start.1 = (f32[128]{0:T(128)S(1)}, f32[128]{0:T(128)}, u32[]{:S(2)}) copy-start(f32[128]{0:T(128)} %param.10) | copy-start | bytes 1540
  83.9 20.6 %collective-permute-start = (bf16[128,1024]{1,0:T(8,128)(2,1)S(1)}, bf16[128,1024]{1,0:T(8,128)(2,1)S(1)}, u32[]{:S(2)}, u32[]{:S(2)}) collective-permute-start(bf16[128,1024]{1,0:T(8,128)(2,1)S(1)} %reshape.117), channel_id=1, source_target_pairs={{0,12},{4,16},{8,20},{12,24},{16,28},{20,32},{24,36},{28,40},{32,4... | collective-permute-start | bytes 786440 | tf_op jit(solution)/shard_map/ppermute | solution.py:14
  104.5 8.3 %collective-permute-start.1 = (bf16[128,1024]{1,0:T(8,128)(2,1)S(1)}, bf16[128,1024]{1,0:T(8,128)(2,1)S(1)}, u32[]{:S(2)}, u32[]{:S(2)}) collective-permute-start(bf16[128,1024]{1,0:T(8,128)(2,1)S(1)} %collective-permute-done), channel_id=1, source_target_pairs={{0,508},{4,0},{8,4},{12,8},{16,12},{20,16},{24,20},{28,24},{32,28}... | collective-permute-start | bytes 786440 | tf_op jit(solution)/shard_map/ppermute | solution.py:14
  112.7 7.7 %collective-permute-start.2 = (bf16[128,1024]{1,0:T(8,128)(2,1)S(1)}, bf16[128,1024]{1,0:T(8,128)(2,1)S(1)}, u32[]{:S(2)}, u32[]{:S(2)}) collective-permute-start(bf16[128,1024]{1,0:T(8,128)(2,1)S(1)} %collective-permute-done.1), channel_id=1, source_target_pairs={{0,508},{4,0},{8,4},{12,8},{16,12},{20,16},{24,20},{28,24},{32,28}... | collective-permute-start | bytes 786440 | tf_op jit(solution)/shard_map/ppermute | solution.py:14
  120.4 7.7 %collective-permute-start.3 = (bf16[128,1024]{1,0:T(8,128)(2,1)S(1)}, bf16[128,1024]{1,0:T(8,128)(2,1)S(1)}, u32[]{:S(2)}, u32[]{:S(2)}) collective-permute-start(bf16[128,1024]{1,0:T(8,128)(2,1)S(1)} %collective-permute-done.2), channel_id=1, source_target_pairs={{0,508},{4,0},{8,4},{12,8},{16,12},{20,16},{24,20},{28,24},{32,28}... | collective-permute-start | bytes 786440 | tf_op jit(solution)/shard_map/ppermute | solution.py:14
  128.1 15.8 %collective-permute-start.4 = (bf16[128,1024]{1,0:T(8,128)(2,1)S(1)}, bf16[128,1024]{1,0:T(8,128)(2,1)S(1)}, u32[]{:S(2)}, u32[]{:S(2)}) collective-permute-start(bf16[128,1024]{1,0:T(8,128)(2,1)S(1)} %collective-permute-done.3), channel_id=1, source_target_pairs={{0,508},{4,0},{8,4},{12,8},{16,12},{20,16},{24,20},{28,24},{32,28}... | collective-permute-start | bytes 786440 | tf_op jit(solution)/shard_map/ppermute | solution.py:14
  143.8 18.6 %collective-permute-start.5 = (bf16[128,1024]{1,0:T(8,128)(2,1)S(1)}, bf16[128,1024]{1,0:T(8,128)(2,1)S(1)}, u32[]{:S(2)}, u32[]{:S(2)}) collective-permute-start(bf16[128,1024]{1,0:T(8,128)(2,1)S(1)} %collective-permute-done.4), channel_id=1, source_target_pairs={{0,508},{4,0},{8,4},{12,8},{16,12},{20,16},{24,20},{28,24},{32,28}... | collective-permute-start | bytes 786440 | tf_op jit(solution)/shard_map/ppermute | solution.py:14
  162.5 17.5 %collective-permute-start.6 = (bf16[128,1024]{1,0:T(8,128)(2,1)S(1)}, bf16[128,1024]{1,0:T(8,128)(2,1)S(1)}, u32[]{:S(2)}, u32[]{:S(2)}) collective-permute-start(bf16[128,1024]{1,0:T(8,128)(2,1)S(1)} %collective-permute-done.5), channel_id=1, source_target_pairs={{0,508},{4,0},{8,4},{12,8},{16,12},{20,16},{24,20},{28,24},{32,28}... | collective-permute-start | bytes 786440 | tf_op jit(solution)/shard_map/ppermute | solution.py:14
  180.0 16.0 %collective-permute-start.7 = (bf16[128,1024]{1,0:T(8,128)(2,1)S(1)}, bf16[128,1024]{1,0:T(8,128)(2,1)S(1)}, u32[]{:S(2)}, u32[]{:S(2)}) collective-permute-start(bf16[128,1024]{1,0:T(8,128)(2,1)S(1)} %collective-permute-done.6), channel_id=1, source_target_pairs={{0,508},{4,0},{8,4},{12,8},{16,12},{20,16},{24,20},{28,24},{32,28}... | collective-permute-start | bytes 786440 | tf_op jit(solution)/shard_map/ppermute | solution.py:14
Sparse Core Ops, SparseCore 0:
  199.7 81.0 reduce-scatter.1
where the time goes:
time: 291 us; the launch traced here: 290 us
  waiting for transfers between devices  154 us (53%)
  starting transfers between devices  104 us (36%)
  between operations  13.7 us (5%)
  local copies, waits for them, and re-layouts  10 us (3%)
  other arithmetic  4.21 us (1%)
  matrix products  3.76 us (1%)
    reduce_scatter x1, waiting for transfers between devices, shards(): lax.psum_scatter(tiles.reshape(freq_count, row_count, -1), 'pair', scatte...  81.2 us
    ppermute x8, starting transfers between devices, from_behind(): lax.ppermute(x, axis, [(i, (i + by) % devices) for i in range(devices)])  77.4 us
    ppermute x8, waiting for transfers between devices, from_behind(): lax.ppermute(x, axis, [(i, (i + by) % devices) for i in range(devices)])  34.2 us
    all_to_all x1, waiting for transfers between devices, shards(): lax.all_to_all(outgoing, 'blk', split_axis=0, concat_axis=0, tiled=True)  28.1 us
    all_to_all x1, starting transfers between devices, shards(): lax.all_to_all(landing, 'blk', split_axis=0, concat_axis=0, tiled=True)  20.9 us
    all_to_all x1, waiting for transfers between devices, shards(): lax.all_to_all(landing, 'blk', split_axis=0, concat_axis=0, tiled=True)  10.1 us
    all_to_all x1, starting transfers between devices, shards(): lax.all_to_all(outgoing, 'blk', split_axis=0, concat_axis=0, tiled=True)  6.12 us
  transfers between devices with their start and end apart: 11, of which 11 were waited for; matrix products, arithmetic and copies ran while one was open for 2% of the time, Pallas kernels for 0%

commit v1 on v0

v1 whole, which is shorter than its diff:
```python
import functools

import jax
import jax.numpy as jnp
from jax import lax
from jax.experimental import pallas as pl
from jax.experimental.pallas import tpu as pltpu
from jax.sharding import PartitionSpec as P

MESH = pl.DeviceIdType.MESH
GRID = 32
STEPS = 8


def route_kernel(chips, depth, ids_ref, out_ref, got_ref, all_ids_ref, staged, arrived, ids, pair_sem, sems):
    blk, pair = lax.axis_index("blk"), lax.axis_index("pair")
    chip, core = blk // 2, lax.rem(blk, 2)
    upper, low = chip // depth, lax.rem(chip, depth)
    uppers = chips // depth
    sibling = (chip * 2 + 1 - core, pair)

    def same_core(other):
        return (other * 2 + core, pair)

    barrier = pltpu.get_barrier_semaphore()
    pl.semaphore_signal(barrier, inc=1, device_id=sibling, device_id_type=MESH)

    def greet(i, carry):
        pl.semaphore_signal(
            barrier, inc=1, device_id=same_core(lax.rem(chip + i, chips)), device_id_type=MESH
        )
        return carry

    lax.fori_loop(1, chips, greet, 0)
    pl.semaphore_wait(barrier, chips)

    ids[upper, low, core] = ids_ref[...]
    swap_ids = pltpu.make_async_remote_copy(
        ids.at[upper, low, core],
        ids.at[upper, low, core],
        pair_sem.at[0],
        pair_sem.at[1],
        device_id=sibling,
        device_id_type=MESH,
    )
    swap_ids.start()
    swap = pltpu.make_async_remote_copy(
        out_ref.at[1 - core],
        staged.at[:, core],
        pair_sem.at[2],
        pair_sem.at[3],
        device_id=sibling,
        device_id_type=MESH,
    )
    swap.start()
    staged[:, core] = out_ref[core]
    swap_ids.wait()
    for i in range(1, depth):
        pltpu.make_async_remote_copy(
            ids.at[upper, low],
            ids.at[upper, low],
            sems.at[0],
            sems.at[1],
            device_id=same_core(upper * depth + lax.rem(low + i, depth)),
            device_id_type=MESH,
        ).start()
    swap.wait()

    def send(i, carry):
        other = lax.rem(chip + i * 27, chips)
        pltpu.make_async_remote_copy(
            staged.at[other],
            arrived.at[chip],
            sems.at[2],
            sems.at[3],
            device_id=same_core(other),
            device_id_type=MESH,
        ).start()
        return carry

    lax.fori_loop(1, chips, send, 0)
    arrived[chip] = staged[chip]
    low_part = ids.at[0, pl.ds(0, depth - 1)]
    pltpu.make_async_remote_copy(
        low_part, low_part, sems.at[0], sems.at[1], device_id=sibling, device_id_type=MESH
    ).wait()
    for i in range(1, uppers):
        pltpu.make_async_remote_copy(
            ids.at[upper],
            ids.at[upper],
            sems.at[4],
            sems.at[5],
            device_id=same_core(lax.rem(upper + i, uppers) * depth + low),
            device_id_type=MESH,
        ).start()
    upper_part = ids.at[pl.ds(0, uppers - 1)]
    pltpu.make_async_remote_copy(
        upper_part, upper_part, sems.at[4], sems.at[5], device_id=sibling, device_id_type=MESH
    ).wait()
    all_ids_ref[...] = ids[...]
    most = arrived.at[pl.ds(0, chips - 1)]
    pltpu.make_async_remote_copy(
        most, most, sems.at[2], sems.at[3], device_id=sibling, device_id_type=MESH
    ).wait()
    got_ref[...] = arrived[...]


def band_kernel(
    chips, own_ref, factor_ref, result_ref, halo, weighted, partial, outbox, inbox,
    halo_send, halo_recv, core_send, core_recv, part_send, part_recv
):
    blk, pair = lax.axis_index("blk"), lax.axis_index("pair")
    pairs = 4
    chip, core = blk // 2, lax.rem(blk, 2)
    above = (lax.rem(chip + 1, chips) * 2 + core, pair)
    below = (lax.rem(chip + chips - 1, chips) * 2 + core, pair)
    sibling = (chip * 2 + 1 - core, pair)
    freqs = factor_ref.shape[0]
    rows = own_ref.shape[0]

    barrier = pltpu.get_barrier_semaphore()
    for other in (above, below, sibling):
        pl.semaphore_signal(barrier, inc=1, device_id=other, device_id_type=MESH)
    for i in range(1, pairs):
        pl.semaphore_signal(
            barrier, inc=1, device_id=(blk, lax.rem(pair + i, pairs)), device_id_type=MESH
        )
    pl.semaphore_wait(barrier, 3 + pairs - 1)

    def link(source, slot, lane, other):
        return pltpu.make_async_remote_copy(
            source, halo.at[slot], halo_send.at[lane], halo_recv.at[lane], device_id=other, device_id_type=MESH
        )

    def across(source, slot, lane):
        return pltpu.make_async_remote_copy(
            source, halo.at[slot], core_send.at[lane], core_recv.at[lane], device_id=sibling, device_id_type=MESH
        )

    up = link(own_ref, 1 + core, 0, above)
    down = link(own_ref, 5 + core, 1, below)
    beside = across(own_ref, 3 + core, 0)
    down.start()
    up.start()
    beside.start()

    for k in range(freqs):
        weighted[pl.ds(k * rows, rows)] = (
            own_ref[...].astype(jnp.float32) * factor_ref[pl.ds(k, 1)]
        ).astype(jnp.bfloat16)

    def send_part(step, stop):
        return pltpu.make_async_remote_copy(
            outbox.at[step],
            inbox.at[pair, lax.rem(stop, 2)],
            part_send.at[step],
            part_recv.at[pair, lax.rem(stop, 2)],
            device_id=(blk, stop // 2),
            device_id_type=MESH,
        )

    def tile(step, stop, block):
        value = lax.dot_general(
            weighted[...], block, (((1,), (1,)), ((), ())), preferred_element_type=jnp.float32
        )

        @pl.when(stop // 2 == pair)
        def _():
            partial[lax.rem(stop, 2)] = value

        @pl.when(stop // 2 != pair)
        def _():
            outbox[step] = value.astype(jnp.bfloat16)
            send_part(step, stop).start()

    stops = (3, 4 - 2 * core, 1, 5, 2 - 2 * core, 6 - 2 * core, 6 * core, 7)
    tile(0, stops[0], own_ref[...])
    beside.wait_recv()
    tile(1, stops[1], halo[4 - core])
    down.wait_recv()
    down2 = link(halo.at[5 + core], 7 + core, 2, below)
    down2.start()
    cross_down = across(halo.at[5 + core], 5 + core, 1)
    cross_down.start()
    up.wait_recv()
    up2 = link(halo.at[2], 0, 3, above)

    @pl.when(core == 1)
    def _():
        up2.start()

    cross_up = across(halo.at[1 + core], 1 + core, 2)
    cross_up.start()
    tile(2, stops[2], halo[1 + core])
    tile(3, stops[3], halo[5 + core])
    cross_up.wait_recv()
    tile(4, stops[4], halo[2 - core])
    cross_down.wait_recv()
    tile(5, stops[5], halo[6 - core])
    last = across(halo.at[7 - 7 * core], 7 - 7 * core, 3)
    down2.wait_recv()

    @pl.when(core == 0)
    def _():
        last.start()

    tile(7, stops[7], halo[7 + core])

    @pl.when(core == 1)
    def _():
        up2.wait_recv()
        last.start()

    last.wait_recv()
    tile(6, stops[6], halo[7 * core])

    for copy in (up, down, down2, beside, cross_up, cross_down, last):
        copy.wait_send()

    @pl.when(core == 1)
    def _():
        up2.wait_send()

    for i in range(1, pairs):
        other = lax.rem(pair + i, pairs)
        for half in range(2):
            pltpu.make_async_remote_copy(
                outbox.at[0],
                inbox.at[other, half],
                part_send.at[0],
                part_recv.at[other, half],
                device_id=(blk, other),
                device_id_type=MESH,
            ).wait_recv()
    for step in range(STEPS):

        @pl.when(stops[step] // 2 != pair)
        def _():
            send_part(step, stops[step]).wait_send()

    scaling = 1.0 / 64.0
    for half in range(2):
        total = partial[half]
        for i in range(1, pairs):
            total = total + inbox[lax.rem(pair + i, pairs), half].astype(jnp.float32)
        result_ref[:, :, half * rows : (half + 1) * rows] = (total * scaling).reshape(freqs, rows, rows)


def response_factor(occ_values, vir_values, frequency):
    gap = vir_values[None, :] - occ_values[:, None]
    factor = 2.0 * gap[None] / (gap[None] * gap[None] + (frequency * frequency)[:, None, None])
    return factor.reshape(frequency.shape[0], -1)


def shards(half_blocks, row_target, vir_coeff, occ_energy, vir_energy, freq_pick):
    devices = lax.axis_size("blk")
    chips = devices // 2
    rows, occ, basis = half_blocks.shape
    virtual = vir_coeff.shape[1]
    width = occ * virtual
    freqs = freq_pick.shape[0]
    row_ids = jnp.arange(rows, dtype=jnp.int32)

    virt = jnp.dot(
        half_blocks.reshape(rows * occ, basis), vir_coeff, preferred_element_type=jnp.float32
    ).astype(jnp.bfloat16)
    owner = row_target // rows
    alike = owner[:, None] == owner[None, :]
    rank = jnp.sum((alike & (row_ids[None, :] < row_ids[:, None])).astype(jnp.int32), axis=1)
    slot = lax.rem(owner, 2) * devices + (owner // 2) * 2 + rank
    slots = jnp.arange(2 * devices, dtype=jnp.int32)
    pick = (slots[:, None] == slot[None, :]).astype(jnp.bfloat16)
    outgoing = jnp.dot(pick, virt.reshape(rows, width), preferred_element_type=jnp.float32)
    outgoing = outgoing.astype(jnp.bfloat16).reshape(2, chips, 2 * occ, virtual)

    depth = 8
    vmem = pl.BlockSpec(memory_space=pltpu.VMEM)
    got, ids = pl.pallas_call(
        functools.partial(route_kernel, chips, depth),
        out_shape=(
            jax.ShapeDtypeStruct((chips, 2, 2 * occ, virtual), jnp.bfloat16),
            jax.ShapeDtypeStruct((chips // depth, depth, 2, 1, rows), jnp.int32),
        ),
        in_specs=[vmem, vmem],
        out_specs=(vmem, vmem),
        scratch_shapes=[
            pltpu.VMEM((chips, 2, 2 * occ, virtual), jnp.bfloat16),
            pltpu.VMEM((chips, 2, 2 * occ, virtual), jnp.bfloat16),
            pltpu.VMEM((chips // depth, depth, 2, 1, rows), jnp.int32),
            pltpu.SemaphoreType.DMA((4,)),
            pltpu.SemaphoreType.DMA((6,)),
        ],
        compiler_params=pltpu.CompilerParams(
            collective_id=0, has_side_effects=True, vmem_limit_bytes=32 * 2**20
        ),
        name="route",
    )(row_target.reshape(1, rows), outgoing)

    ids = ids.reshape(devices, rows)
    mine = (ids // rows) == lax.axis_index("blk")
    earlier = (row_ids[:, None] < row_ids[None, :]).astype(jnp.bfloat16)
    order = jnp.dot(mine.astype(jnp.bfloat16), earlier, preferred_element_type=jnp.float32)
    place = lax.rem(ids, rows) + 1
    landing = jnp.stack(
        [jnp.sum(jnp.where(mine & (order == k), place, 0), axis=1) for k in range(2)], axis=1
    ).reshape(2 * devices)
    put = (row_ids[:, None] + 1 == landing[None, :]).astype(jnp.bfloat16)
    own = jnp.dot(
        put, got.reshape(2 * devices, width), preferred_element_type=jnp.float32
    ).astype(jnp.bfloat16)

    frequency = 0.5 * jnp.tan(jnp.pi * (freq_pick.astype(jnp.float32) + 0.5) / (2.0 * GRID))
    own_occ = lax.dynamic_slice_in_dim(occ_energy, lax.axis_index("pair") * occ, occ)
    factor = response_factor(own_occ, vir_energy, frequency)

    return pl.pallas_call(
        functools.partial(band_kernel, chips),
        out_shape=jax.ShapeDtypeStruct((freqs, rows, 2 * rows), jnp.float32),
        in_specs=[vmem, vmem],
        out_specs=vmem,
        scratch_shapes=[
            pltpu.VMEM((9, rows, width), jnp.bfloat16),
            pltpu.VMEM((freqs * rows, width), jnp.bfloat16),
            pltpu.VMEM((2, freqs * rows, rows), jnp.float32),
            pltpu.VMEM((STEPS, freqs * rows, rows), jnp.bfloat16),
            pltpu.VMEM((4, 2, freqs * rows, rows), jnp.bfloat16),
            pltpu.SemaphoreType.DMA((4,)),
            pltpu.SemaphoreType.DMA((4,)),
            pltpu.SemaphoreType.DMA((4,)),
            pltpu.SemaphoreType.DMA((4,)),
            pltpu.SemaphoreType.DMA((STEPS,)),
            pltpu.SemaphoreType.DMA((4, 2)),
        ],
        compiler_params=pltpu.CompilerParams(
            collective_id=1, has_side_effects=True, vmem_limit_bytes=48 * 2**20
        ),
        name="band",
    )(own, factor)


def solution(mesh):
    return jax.shard_map(
        shards,
        mesh=mesh,
        in_specs=(P("blk", "pair", None), P("blk"), P(), P(), P(), P()),
        out_specs=P(None, "blk", "pair"),
        check_vma=False,
    )
```

time: 291 us -> 107 us (0.37)
  waiting for transfers between devices: 154 us -> 0 us
  starting transfers between devices: 104 us -> 0 us
  Pallas kernels: 0 us -> 102 us
  between operations: 13.7 us -> 0.13 us
  local copies, waits for them, and re-layouts: 10 us -> 3.84 us
  other arithmetic: 4.21 us -> 0.35 us
    pallas_call x0 -> x2, Pallas kernels: none -> 102 us  [the longest x1 66.6 us: shards(): pl.pallas_call(functools.partial(band_kernel, chips), out_shape=jax.Shape...]
    reduce_scatter x1 -> x0, waiting for transfers between devices: 81.2 us -> none  [shards(): lax.psum_scatter(tiles.reshape(freq_count, row_count, -1), 'pair', scatte...]
    ppermute x8 -> x0, starting transfers between devices: 77.4 us -> none  [from_behind(): lax.ppermute(x, axis, [(i, (i + by) % devices) for i in range(devices)])]
    all_to_all x2 -> x0, waiting for transfers between devices: 38.2 us -> none  [the longest x1 28.1 us: shards(): lax.all_to_all(outgoing, 'blk', split_axis=0, concat_axis=0, tiled=True)]
    ppermute x8 -> x0, waiting for transfers between devices: 34.2 us -> none  [from_behind(): lax.ppermute(x, axis, [(i, (i + by) % devices) for i in range(devices)])]
    all_to_all x2 -> x0, starting transfers between devices: 27 us -> none  [the longest x1 20.9 us: shards(): lax.all_to_all(landing, 'blk', split_axis=0, concat_axis=0, tiled=True)]
    scatter x3 -> x0, local copies, waits for them, and re-layouts: 4.87 us -> none  [the longest x1 2.19 us: put_rows(): return empty.at[safe_ids].set(arrived, mode='drop')]
    all_to_all x5 -> x0, local copies, waits for them, and re-layouts: 3.33 us -> none  [the longest x2 1.91 us: shards(): lax.all_to_all(outgoing, 'blk', split_axis=0, concat_axis=0, tiled=True)]
  transfers between devices with their start and end apart: 11 -> 0, of which waited for: 11 -> 0; matrix products, arithmetic and copies ran while one was open for 2% -> 0% of each run, Pallas kernels for 0% -> 0%
where the time goes in v1:
time: 107 us
  Pallas kernels  102 us (95%)
  local copies, waits for them, and re-layouts  3.84 us (4%)
  matrix products  1.09 us (1%)
    pallas_call x1, Pallas kernels, shards(): pl.pallas_call(functools.partial(band_kernel, chips), out_shape=jax.Shape...  66.6 us
    pallas_call x1, Pallas kernels, shards(): pl.pallas_call(functools.partial(route_kernel, chips, depth), out_shape=(...  34.9 us
    unnamed x13, local copies, waits for them, and re-layouts  2.79 us

profile of v1, /device:TPU:1, one launch (start us, length us, event | category | flops | bytes accessed | tf_op | source)
XLA Modules:
  0.0 106.9 jit_solution(12020537317102212351)
XLA Ops:
  0.0 0.0 copy-start
  0.0 0.0 copy-start.4
  0.0 0.7 copy-done.4
  0.7 0.0 copy-start.5
  0.7 0.0 copy-start.3
  0.7 0.1 dynamic_slice.3
  0.8 0.6 copy-done.5
  1.4 0.0 copy-start.1
  1.4 0.0 copy-start.2
  1.4 0.6 copy-done.1
  2.0 0.2 convert_reduce_fusion
  2.3 0.1 sub.45
  2.3 0.0 copy-done.3
  2.3 0.1 add_divide_fusion.factor_ref
  2.4 0.0 copy-done
  2.4 0.0 copy-done.2
  2.4 0.3 convolution_convert_fusion.2
  2.7 0.1 reshape.79
  2.9 0.3 convolution_convert_fusion
  3.2 0.2 reshape.80.out_ref
  3.4 34.9 %route.1 = (bf16[64,2,16,128]{3,2,1,0:T(8,128)(2,1)S(1)}, s32[8,8,2,1,128]{4,3,2,1,0:T(1,128)S(1)}) custom-call(s32[1,128]{1,0:T(1,128)S(1)} %bitcast.20, bf16[2,64,16,128]{3,2,1,0:T(8,128)(2,1)S(1)} %reshape.80.out_ref), custom_call_target="tpu_custom_call" | custom-call | tf_op jit(solution)/shard_map/route/pallas_call | solution.py:278
  38.3 0.1 copy.16
  38.4 0.2 select_reduce_fusion.1
  38.7 0.1 copy.20
  38.8 0.1 eq.72
  38.9 0.2 reshape.82
  39.2 0.3 convolution_convert_fusion.1.own_ref
  39.4 66.6 %band.1 = f32[6,128,256]{2,1,0:T(8,128)S(1)} custom-call(bf16[128,1024]{1,0:T(8,128)(2,1)S(1)} %convolution_convert_fusion.1.own_ref, f32[6,1024]{1,0:T(8,128)S(1)} %add_divide_fusion.factor_ref), custom_call_target="tpu_custom_call" | custom-call | tf_op jit(solution)/shard_map/band/pallas_call | solution.py:316
  106.1 0.9 copy.22
  (6 shorter events, 0.1 us)
Async XLA Ops:
  0.0 2.4 %copy-start = (bf16[128,8,256]{2,1,0:T(8,128)(2,1)S(1)}, bf16[128,8,256]{2,1,0:T(8,128)(2,1)}, u32[]{:S(2)}) copy-start(bf16[128,8,256]{2,1,0:T(8,128)(2,1)} %param.6) | copy-start | bytes 1572868
  0.0 0.7 copy-start.4
  0.7 0.7 copy-start.5
  0.7 1.6 %copy-start.3 = (f32[128]{0:T(128)S(1)}, f32[128]{0:T(128)}, u32[]{:S(2)}) copy-start(f32[128]{0:T(128)} %param.10) | copy-start | bytes 1540
  1.4 0.7 copy-start.1
  1.4 1.1 copy-start.2

commit v2 on v1

--- a/solution.py
+++ b/solution.py
@@ -106,26 +106,30 @@
 
 
 def band_kernel(
-    chips, own_ref, factor_ref, result_ref, halo, weighted, partial, outbox, inbox,
+    chips, depth, own_ref, factor_ref, result_ref, halo, weighted, partial, outbox, inbox,
     halo_send, halo_recv, core_send, core_recv, part_send, part_recv
 ):
     blk, pair = lax.axis_index("blk"), lax.axis_index("pair")
     pairs = 4
     chip, core = blk // 2, lax.rem(blk, 2)
-    above = (lax.rem(chip + 1, chips) * 2 + core, pair)
-    below = (lax.rem(chip + chips - 1, chips) * 2 + core, pair)
+    low = lax.rem(chip, depth)
+
+    def along(by):
+        return (lax.rem(chip + chips + by, chips) * 2 + core, pair)
+
+    above, below = along(1), along(-1)
     sibling = (chip * 2 + 1 - core, pair)
     freqs = factor_ref.shape[0]
     rows = own_ref.shape[0]
 
     barrier = pltpu.get_barrier_semaphore()
-    for other in (above, below, sibling):
+    for other in (above, below, along(2), along(-2), sibling):
         pl.semaphore_signal(barrier, inc=1, device_id=other, device_id_type=MESH)
     for i in range(1, pairs):
         pl.semaphore_signal(
             barrier, inc=1, device_id=(blk, lax.rem(pair + i, pairs)), device_id_type=MESH
         )
-    pl.semaphore_wait(barrier, 3 + pairs - 1)
+    pl.semaphore_wait(barrier, 5 + pairs - 1)
 
     def link(source, slot, lane, other):
         return pltpu.make_async_remote_copy(
@@ -140,9 +144,22 @@
     up = link(own_ref, 1 + core, 0, above)
     down = link(own_ref, 5 + core, 1, below)
     beside = across(own_ref, 3 + core, 0)
+    def far(slot, lane, receive, other):
+        return pltpu.make_async_remote_copy(
+            own_ref, halo.at[slot], halo_send.at[lane], halo_recv.at[receive], device_id=other, device_id_type=MESH
+        )
+
+    far_down_own = far(7 + core, 4, 2, along(-2))
+    far_up_own = far(0, 5, 3, along(2))
+    serves_down, serves_up = low == 1, (low == depth - 2) & (core == 1)
+    hands_down, hands_up = low != 0, (low != depth - 1) & (core == 1)
     down.start()
     up.start()
     beside.start()
+
+    pl.when(serves_down)(far_down_own.start)
+
+    pl.when(serves_up)(far_up_own.start)
 
     for k in range(freqs):
         weighted[pl.ds(k * rows, rows)] = (
@@ -179,13 +196,17 @@
     tile(1, stops[1], halo[4 - core])
     down.wait_recv()
     down2 = link(halo.at[5 + core], 7 + core, 2, below)
-    down2.start()
+
+    @pl.when(hands_down)
+    def _():
+        down2.start()
+
     cross_down = across(halo.at[5 + core], 5 + core, 1)
     cross_down.start()
     up.wait_recv()
     up2 = link(halo.at[2], 0, 3, above)
 
-    @pl.when(core == 1)
+    @pl.when(hands_up)
     def _():
         up2.start()
 
@@ -214,12 +235,12 @@
     last.wait_recv()
     tile(6, stops[6], halo[7 * core])
 
-    for copy in (up, down, down2, beside, cross_up, cross_down, last):
+    for copy in (up, down, beside, cross_up, cross_down, last):
         copy.wait_send()
-
-    @pl.when(core == 1)
-    def _():
-        up2.wait_send()
+    for taken, copy in (
+        (hands_down, down2), (hands_up, up2), (serves_down, far_down_own), (serves_up, far_up_own)
+    ):
+        pl.when(taken)(copy.wait_send)
 
     for i in range(1, pairs):
         other = lax.rem(pair + i, pairs)
@@ -314,7 +335,7 @@
     factor = response_factor(own_occ, vir_energy, frequency)
 
     return pl.pallas_call(
-        functools.partial(band_kernel, chips),
+        functools.partial(band_kernel, chips, depth),
         out_shape=jax.ShapeDtypeStruct((freqs, rows, 2 * rows), jnp.float32),
         in_specs=[vmem, vmem],
         out_specs=vmem,
@@ -324,7 +345,7 @@
             pltpu.VMEM((2, freqs * rows, rows), jnp.float32),
             pltpu.VMEM((STEPS, freqs * rows, rows), jnp.bfloat16),
             pltpu.VMEM((4, 2, freqs * rows, rows), jnp.bfloat16),
-            pltpu.SemaphoreType.DMA((4,)),
+            pltpu.SemaphoreType.DMA((6,)),
             pltpu.SemaphoreType.DMA((4,)),
             pltpu.SemaphoreType.DMA((4,)),
             pltpu.SemaphoreType.DMA((4,)),

time: 107 us -> 97.7 us (0.913); the launches traced: 107 us -> 95.9 us
  Pallas kernels: 102 us -> 90.4 us
    pallas_call x1, Pallas kernels: 66.6 us -> 55.5 us  [shards(): pl.pallas_call(functools.partial(band_kernel, chips, depth), out_shape=ja...]
where the time goes in v2:
time: 97.7 us; the launch traced here: 95.9 us
  Pallas kernels  90.4 us (93%)
  local copies, waits for them, and re-layouts  3.84 us (4%)
  matrix products  1.09 us (1%)
    pallas_call x1, Pallas kernels, shards(): pl.pallas_call(functools.partial(band_kernel, chips, depth), out_shape=ja...  55.5 us
    pallas_call x1, Pallas kernels, shards(): pl.pallas_call(functools.partial(route_kernel, chips, depth), out_shape=(...  34.9 us
    unnamed x13, local copies, waits for them, and re-layouts  2.79 us

profile of v2, /device:TPU:1, one launch (start us, length us, event | category | flops | bytes accessed | tf_op | source)
XLA Modules:
  0.0 95.9 jit_solution(7193935903189517336)
XLA Ops:
  0.0 0.0 copy-start
  0.0 0.0 copy-start.4
  0.0 0.7 copy-done.4
  0.7 0.0 copy-start.5
  0.7 0.0 copy-start.3
  0.7 0.1 dynamic_slice.3
  0.8 0.6 copy-done.5
  1.4 0.0 copy-start.1
  1.4 0.0 copy-start.2
  1.4 0.6 copy-done.1
  2.0 0.2 convert_reduce_fusion
  2.3 0.1 sub.45
  2.3 0.0 copy-done.3
  2.3 0.1 add_divide_fusion.factor_ref
  2.4 0.0 copy-done
  2.4 0.0 copy-done.2
  2.4 0.3 convolution_convert_fusion.2
  2.7 0.1 reshape.79
  2.9 0.3 convolution_convert_fusion
  3.2 0.2 reshape.80.out_ref
  3.4 34.9 %route.1 = (bf16[64,2,16,128]{3,2,1,0:T(8,128)(2,1)S(1)}, s32[8,8,2,1,128]{4,3,2,1,0:T(1,128)S(1)}) custom-call(s32[1,128]{1,0:T(1,128)S(1)} %bitcast.20, bf16[2,64,16,128]{3,2,1,0:T(8,128)(2,1)S(1)} %reshape.80.out_ref), custom_call_target="tpu_custom_call" | custom-call | tf_op jit(solution)/shard_map/route/pallas_call | solution.py:299
  38.3 0.1 copy.16
  38.4 0.2 select_reduce_fusion.1
  38.7 0.1 copy.20
  38.8 0.1 eq.72
  38.9 0.2 reshape.82
  39.2 0.3 convolution_convert_fusion.1.own_ref
  39.4 55.5 %band.1 = f32[6,128,256]{2,1,0:T(8,128)S(1)} custom-call(bf16[128,1024]{1,0:T(8,128)(2,1)S(1)} %convolution_convert_fusion.1.own_ref, f32[6,1024]{1,0:T(8,128)S(1)} %add_divide_fusion.factor_ref), custom_call_target="tpu_custom_call" | custom-call | tf_op jit(solution)/shard_map/band/pallas_call | solution.py:337
  95.0 0.9 copy.22
  (6 shorter events, 0.1 us)
Async XLA Ops:
  0.0 2.4 %copy-start = (bf16[128,8,256]{2,1,0:T(8,128)(2,1)S(1)}, bf16[128,8,256]{2,1,0:T(8,128)(2,1)}, u32[]{:S(2)}) copy-start(bf16[128,8,256]{2,1,0:T(8,128)(2,1)} %param.6) | copy-start | bytes 1572868
  0.0 0.7 copy-start.4
  0.7 0.7 copy-start.5
  0.7 1.6 %copy-start.3 = (f32[128]{0:T(128)S(1)}, f32[128]{0:T(128)}, u32[]{:S(2)}) copy-start(f32[128]{0:T(128)} %param.10) | copy-start | bytes 1540
  1.4 0.7 copy-start.1
  1.4 1.1 %copy-start.2 = (bf16[256,128]{1,0:T(8,128)(2,1)S(1)}, bf16[256,128]{1,0:T(8,128)(2,1)}, u32[]{:S(2)}) copy-start(bf16[256,128]{1,0:T(8,128)(2,1)} %param.8) | copy-start | bytes 196612

commit v3 on v2

--- a/solution.py
+++ b/solution.py
@@ -106,8 +106,8 @@
 
 
 def band_kernel(
-    chips, depth, own_ref, factor_ref, result_ref, halo, weighted, partial, outbox, inbox,
-    halo_send, halo_recv, core_send, core_recv, part_send, part_recv
+    chips, depth, own_ref, occ_ref, vir_ref, pick_ref, result_ref, halo, weighted, partial, outbox, inbox,
+    joint, relayed, halo_send, halo_recv, core_send, core_recv, part_send, part_recv, relay_send, relay_recv
 ):
     blk, pair = lax.axis_index("blk"), lax.axis_index("pair")
     pairs = 4
@@ -119,8 +119,10 @@
 
     above, below = along(1), along(-1)
     sibling = (chip * 2 + 1 - core, pair)
-    freqs = factor_ref.shape[0]
-    rows = own_ref.shape[0]
+    freqs = pick_ref.shape[0]
+    rows, width = own_ref.shape
+    virtual = vir_ref.shape[1]
+    occ = width // virtual
 
     barrier = pltpu.get_barrier_semaphore()
     for other in (above, below, along(2), along(-2), sibling):
@@ -129,8 +131,6 @@
         pl.semaphore_signal(
             barrier, inc=1, device_id=(blk, lax.rem(pair + i, pairs)), device_id_type=MESH
         )
-    pl.semaphore_wait(barrier, 5 + pairs - 1)
-
     def link(source, slot, lane, other):
         return pltpu.make_async_remote_copy(
             source, halo.at[slot], halo_send.at[lane], halo_recv.at[lane], device_id=other, device_id_type=MESH
@@ -153,6 +153,110 @@
     far_up_own = far(0, 5, 3, along(2))
     serves_down, serves_up = low == 1, (low == depth - 2) & (core == 1)
     hands_down, hands_up = low != 0, (low != depth - 1) & (core == 1)
+    outer = (pair == 0) | (pair == pairs - 1)
+    inner = jnp.logical_not(outer)
+    beside_me, opposite = 1 + pair // 2, (pairs - 1 - pair) // 2
+
+    def across_middle(stop):
+        return stop // 4 == opposite
+
+    def via(stop):
+        return outer & across_middle(stop)
+
+    def joins(stop):
+        return inner & across_middle(stop)
+
+    def direct(stop):
+        return (stop // 2 != pair) & jnp.logical_not(across_middle(stop))
+
+    def part(slot, stop):
+        half = lax.rem(stop, 2)
+        return pltpu.make_async_remote_copy(
+            outbox.at[slot],
+            inbox.at[pair, half],
+            part_send.at[slot],
+            part_recv.at[pair, half],
+            device_id=(blk, stop // 2),
+            device_id_type=MESH,
+        )
+
+    def send_part(step, stop):
+        return part(step, stop)
+
+    def send_joint(stop):
+        return part(STEPS + lax.rem(stop, 4), stop)
+
+    def send_on(step, stop):
+        which = lax.rem(stop, 4)
+        return pltpu.make_async_remote_copy(
+            outbox.at[step],
+            relayed.at[which],
+            relay_send.at[which],
+            relay_recv.at[which],
+            device_id=(blk, beside_me),
+            device_id_type=MESH,
+        )
+
+    def product(block):
+        return lax.dot_general(
+            weighted[...], block, (((1,), (1,)), ((), ())), preferred_element_type=jnp.float32
+        )
+
+    def keep(step, stop, value):
+        half = lax.rem(stop, 2)
+
+        @pl.when(stop // 2 == pair)
+        def _():
+            partial[half] = value
+
+        @pl.when(joins(stop))
+        def _():
+            joint[lax.rem(stop, 4)] = value
+
+        @pl.when(direct(stop) | via(stop))
+        def _():
+            outbox[step] = value.astype(jnp.bfloat16)
+
+    def dispatch(step, stop):
+        pl.when(direct(stop))(send_part(step, stop).start)
+        pl.when(via(stop))(send_on(step, stop).start)
+
+    def tile(step, stop, block):
+        keep(step, stop, product(block))
+        dispatch(step, stop)
+
+    def tiles(steps, blocks):
+        both = product(jnp.concatenate(blocks, axis=0))
+        for n, step in enumerate(steps):
+            keep(step, stops[step], both[:, n * rows : (n + 1) * rows])
+            dispatch(step, stops[step])
+
+    def join(step):
+        stop = stops[step]
+        which = lax.rem(stop, 4)
+
+        @pl.when(joins(stop))
+        def _():
+            pltpu.make_async_remote_copy(
+                outbox.at[0], relayed.at[which], relay_send.at[which], relay_recv.at[which],
+                device_id=(blk, pairs - 1 - pair), device_id_type=MESH,
+            ).wait_recv()
+            outbox[STEPS + which] = (joint[which] + relayed[which].astype(jnp.float32)).astype(jnp.bfloat16)
+            send_joint(stop).start()
+
+    stops = (3, 4 - 2 * core, 1, 5, 2 - 2 * core, 6 - 2 * core, 6 * core, 7)
+    for k in range(freqs):
+        picked = jnp.full((1, virtual), pick_ref[k], jnp.int32).astype(jnp.float32)
+        frequency = 0.5 * jnp.tan(jnp.pi * (picked + 0.5) / (2.0 * GRID))
+        for i in range(occ):
+            gap = vir_ref[...] - occ_ref[pair * occ + i]
+            factor = 2.0 * gap / (gap * gap + frequency * frequency)
+            lanes = slice(i * virtual, (i + 1) * virtual)
+            weighted[k * rows : (k + 1) * rows, lanes] = (
+                own_ref[:, lanes].astype(jnp.float32) * factor
+            ).astype(jnp.bfloat16)
+    keep(0, stops[0], product(own_ref[...]))
+    pl.semaphore_wait(barrier, 5 + pairs - 1)
     down.start()
     up.start()
     beside.start()
@@ -160,38 +264,7 @@
     pl.when(serves_down)(far_down_own.start)
 
     pl.when(serves_up)(far_up_own.start)
-
-    for k in range(freqs):
-        weighted[pl.ds(k * rows, rows)] = (
-            own_ref[...].astype(jnp.float32) * factor_ref[pl.ds(k, 1)]
-        ).astype(jnp.bfloat16)
-
-    def send_part(step, stop):
-        return pltpu.make_async_remote_copy(
-            outbox.at[step],
-            inbox.at[pair, lax.rem(stop, 2)],
-            part_send.at[step],
-            part_recv.at[pair, lax.rem(stop, 2)],
-            device_id=(blk, stop // 2),
-            device_id_type=MESH,
-        )
-
-    def tile(step, stop, block):
-        value = lax.dot_general(
-            weighted[...], block, (((1,), (1,)), ((), ())), preferred_element_type=jnp.float32
-        )
-
-        @pl.when(stop // 2 == pair)
-        def _():
-            partial[lax.rem(stop, 2)] = value
-
-        @pl.when(stop // 2 != pair)
-        def _():
-            outbox[step] = value.astype(jnp.bfloat16)
-            send_part(step, stop).start()
-
-    stops = (3, 4 - 2 * core, 1, 5, 2 - 2 * core, 6 - 2 * core, 6 * core, 7)
-    tile(0, stops[0], own_ref[...])
+    dispatch(0, stops[0])
     beside.wait_recv()
     tile(1, stops[1], halo[4 - core])
     down.wait_recv()
@@ -212,12 +285,12 @@
 
     cross_up = across(halo.at[1 + core], 1 + core, 2)
     cross_up.start()
-    tile(2, stops[2], halo[1 + core])
-    tile(3, stops[3], halo[5 + core])
+    tiles((3, 2), (halo[5 + core], halo[1 + core]))
+    join(0)
+    join(1)
     cross_up.wait_recv()
-    tile(4, stops[4], halo[2 - core])
     cross_down.wait_recv()
-    tile(5, stops[5], halo[6 - core])
+    tiles((5, 4), (halo[6 - core], halo[2 - core]))
     last = across(halo.at[7 - 7 * core], 7 - 7 * core, 3)
     down2.wait_recv()
 
@@ -232,8 +305,14 @@
         up2.wait_recv()
         last.start()
 
+    join(3)
+    join(2)
     last.wait_recv()
     tile(6, stops[6], halo[7 * core])
+    join(5)
+    join(4)
+    join(7)
+    join(6)
 
     for copy in (up, down, beside, cross_up, cross_down, last):
         copy.wait_send()
@@ -242,35 +321,38 @@
     ):
         pl.when(taken)(copy.wait_send)
 
-    for i in range(1, pairs):
-        other = lax.rem(pair + i, pairs)
+    scaling = 1.0 / 64.0
+
+    def collect(hops):
+        for i in hops:
+            other = lax.rem(pair + i, pairs)
+            for half in range(2):
+                pltpu.make_async_remote_copy(
+                    outbox.at[0],
+                    inbox.at[other, half],
+                    part_send.at[0],
+                    part_recv.at[other, half],
+                    device_id=(blk, other),
+                    device_id_type=MESH,
+                ).wait_recv()
         for half in range(2):
-            pltpu.make_async_remote_copy(
-                outbox.at[0],
-                inbox.at[other, half],
-                part_send.at[0],
-                part_recv.at[other, half],
-                device_id=(blk, other),
-                device_id_type=MESH,
-            ).wait_recv()
+            total = partial[half]
+            for i in hops:
+                total = total + inbox[lax.rem(pair + i, pairs), half].astype(jnp.float32)
+            result_ref[:, :, half * rows : (half + 1) * rows] = (total * scaling).reshape(freqs, rows, rows)
+
+    @pl.when(outer)
+    def _():
+        collect((1 + pair // 3, 2 + pair // 3))
+
+    @pl.when(inner)
+    def _():
+        collect((1, 3))
+
     for step in range(STEPS):
-
-        @pl.when(stops[step] // 2 != pair)
-        def _():
-            send_part(step, stops[step]).wait_send()
-
-    scaling = 1.0 / 64.0
-    for half in range(2):
-        total = partial[half]
-        for i in range(1, pairs):
-            total = total + inbox[lax.rem(pair + i, pairs), half].astype(jnp.float32)
-        result_ref[:, :, half * rows : (half + 1) * rows] = (total * scaling).reshape(freqs, rows, rows)
-
-
-def response_factor(occ_values, vir_values, frequency):
-    gap = vir_values[None, :] - occ_values[:, None]
-    factor = 2.0 * gap[None] / (gap[None] * gap[None] + (frequency * frequency)[:, None, None])
-    return factor.reshape(frequency.shape[0], -1)
+        pl.when(direct(stops[step]))(send_part(step, stops[step]).wait_send)
+        pl.when(via(stops[step]))(send_on(step, stops[step]).wait_send)
+        pl.when(joins(stops[step]))(send_joint(stops[step]).wait_send)
 
 
 def shards(half_blocks, row_target, vir_coeff, occ_energy, vir_energy, freq_pick):
@@ -330,33 +412,34 @@
         put, got.reshape(2 * devices, width), preferred_element_type=jnp.float32
     ).astype(jnp.bfloat16)
 
-    frequency = 0.5 * jnp.tan(jnp.pi * (freq_pick.astype(jnp.float32) + 0.5) / (2.0 * GRID))
-    own_occ = lax.dynamic_slice_in_dim(occ_energy, lax.axis_index("pair") * occ, occ)
-    factor = response_factor(own_occ, vir_energy, frequency)
-
+    smem = pl.BlockSpec(memory_space=pltpu.SMEM)
     return pl.pallas_call(
         functools.partial(band_kernel, chips, depth),
         out_shape=jax.ShapeDtypeStruct((freqs, rows, 2 * rows), jnp.float32),
-        in_specs=[vmem, vmem],
+        in_specs=[vmem, smem, vmem, smem],
         out_specs=vmem,
         scratch_shapes=[
             pltpu.VMEM((9, rows, width), jnp.bfloat16),
             pltpu.VMEM((freqs * rows, width), jnp.bfloat16),
             pltpu.VMEM((2, freqs * rows, rows), jnp.float32),
-            pltpu.VMEM((STEPS, freqs * rows, rows), jnp.bfloat16),
+            pltpu.VMEM((STEPS + 4, freqs * rows, rows), jnp.bfloat16),
             pltpu.VMEM((4, 2, freqs * rows, rows), jnp.bfloat16),
+            pltpu.VMEM((4, freqs * rows, rows), jnp.float32),
+            pltpu.VMEM((4, freqs * rows, rows), jnp.bfloat16),
             pltpu.SemaphoreType.DMA((6,)),
             pltpu.SemaphoreType.DMA((4,)),
             pltpu.SemaphoreType.DMA((4,)),
             pltpu.SemaphoreType.DMA((4,)),
-            pltpu.SemaphoreType.DMA((STEPS,)),
+            pltpu.SemaphoreType.DMA((STEPS + 4,)),
             pltpu.SemaphoreType.DMA((4, 2)),
+            pltpu.SemaphoreType.DMA((4,)),
+            pltpu.SemaphoreType.DMA((4,)),
         ],
         compiler_params=pltpu.CompilerParams(
             collective_id=1, has_side_effects=True, vmem_limit_bytes=48 * 2**20
         ),
         name="band",
-    )(own, factor)
+    )(own, occ_energy, vir_energy.reshape(1, virtual), freq_pick)
 
 
 def solution(mesh):

time: 97.7 us -> 92.6 us (0.948); the launches traced: 95.9 us -> 92.4 us
  Pallas kernels: 90.4 us -> 87.1 us
    pallas_call x1, Pallas kernels: 55.5 us -> 52.2 us  [shards(): pl.pallas_call(functools.partial(band_kernel, chips, depth), out_shape=ja...]
    unnamed x13 -> x11, local copies, waits for them, and re-layouts: 2.79 us -> 2.1 us
where the time goes in v3:
time: 92.6 us; the launch traced here: 92.4 us
  Pallas kernels  87.1 us (94%)
  local copies, waits for them, and re-layouts  3.01 us (3%)
  matrix products  1.92 us (2%)
    pallas_call x1, Pallas kernels, shards(): pl.pallas_call(functools.partial(band_kernel, chips, depth), out_shape=ja...  52.2 us
    pallas_call x1, Pallas kernels, shards(): pl.pallas_call(functools.partial(route_kernel, chips, depth), out_shape=(...  34.9 us
    unnamed x11, local copies, waits for them, and re-layouts  2.1 us

profile of v3, /device:TPU:1, one launch (start us, length us, event | category | flops | bytes accessed | tf_op | source)
XLA Modules:
  0.0 92.4 jit_solution(16489869557253312492)
XLA Ops:
  0.0 0.0 copy-start
  0.0 0.0 copy-start.1
  0.0 0.7 copy-done.1
  0.7 0.2 convert_reduce_fusion
  0.9 0.1 copy-done
  1.1 1.1 %convolution_convert_fusion.2 = bf16[1024,128]{1,0:T(8,128)(2,1)S(1)} fusion(bf16[256,128]{1,0:T(8,128)(2,1)} %param.8, bf16[128,8,256]{2,1,0:T(8,128)(2,1)S(1)} %copy-done), kind=kOutput, calls=%fused_computation.2 | convolution fusion | flops 67239936 | bytes 851968 | tf_op jit(solution)/shard_map/dot_general | solution.py:367
  2.2 0.1 reshape.32
  2.3 0.3 convolution_convert_fusion
  2.6 0.2 reshape.33.out_ref
  2.8 34.9 %route.1 = (bf16[64,2,16,128]{3,2,1,0:T(8,128)(2,1)S(1)}, s32[8,8,2,1,128]{4,3,2,1,0:T(1,128)S(1)}) custom-call(s32[1,128]{1,0:T(1,128)S(1)} %bitcast.14, bf16[2,64,16,128]{3,2,1,0:T(8,128)(2,1)S(1)} %reshape.33.out_ref), custom_call_target="tpu_custom_call" | custom-call | tf_op jit(solution)/shard_map/route/pallas_call | solution.py:381
  37.8 0.1 copy.16
  37.9 0.2 select_reduce_fusion.1
  38.1 0.1 copy.20
  38.2 0.1 eq.72
  38.4 0.2 reshape.35
  38.6 0.0 copy-start.2
  38.6 0.0 copy-start.3
  38.6 0.0 copy-start.4
  38.7 0.3 convolution_convert_fusion.1.own_ref
  38.9 0.3 copy-done.2
  39.3 0.0 copy-done.3
  39.3 0.0 copy-done.4
  39.3 52.2 %band.1 = f32[6,128,256]{2,1,0:T(8,128)S(1)} custom-call(bf16[128,1024]{1,0:T(8,128)(2,1)S(1)} %convolution_convert_fusion.1.own_ref, f32[32]{0:T(128)S(1)} %copy-done.2, f32[1,128]{1,0:T(1,128)S(1)} %bitcast.15, s32[6]{0:T(128)S(1)} %copy-done.4), custom_call_target="tpu_custom_call" | custom-call | tf_op jit(solution)/shard_map/band/pallas_call | solution.py:416
  91.5 0.9 copy.22
  (4 shorter events, 0.0 us)
Async XLA Ops:
  0.0 1.1 %copy-start = (bf16[128,8,256]{2,1,0:T(8,128)(2,1)S(1)}, bf16[128,8,256]{2,1,0:T(8,128)(2,1)}, u32[]{:S(2)}) copy-start(bf16[128,8,256]{2,1,0:T(8,128)(2,1)} %param.6) | copy-start | bytes 1572868
  0.0 0.7 copy-start.1
  38.6 0.7 copy-start.2
  38.6 0.7 copy-start.3
  38.6 0.7 copy-start.4

commit v4 on v3

--- a/solution.py
+++ b/solution.py
@@ -125,7 +125,7 @@
     occ = width // virtual
 
     barrier = pltpu.get_barrier_semaphore()
-    for other in (above, below, along(2), along(-2), sibling):
+    for other in (above, below, along(2), along(-2), along(3), along(-3), sibling):
         pl.semaphore_signal(barrier, inc=1, device_id=other, device_id_type=MESH)
     for i in range(1, pairs):
         pl.semaphore_signal(
@@ -144,14 +144,20 @@
     up = link(own_ref, 1 + core, 0, above)
     down = link(own_ref, 5 + core, 1, below)
     beside = across(own_ref, 3 + core, 0)
-    def far(slot, lane, receive, other):
+    def far(source, target, lane, receive, by):
         return pltpu.make_async_remote_copy(
-            own_ref, halo.at[slot], halo_send.at[lane], halo_recv.at[receive], device_id=other, device_id_type=MESH
-        )
-
-    far_down_own = far(7 + core, 4, 2, along(-2))
-    far_up_own = far(0, 5, 3, along(2))
-    serves_down, serves_up = low == 1, (low == depth - 2) & (core == 1)
+            source, target, halo_send.at[lane], halo_recv.at[receive], device_id=along(by), device_id_type=MESH
+        )
+
+    split = rows // 2
+    first, second = pl.ds(0, split), pl.ds(split, rows - split)
+    down_first = far(own_ref.at[first], halo.at[5 + core, first], 1, 1, -1)
+    down_second = far(halo.at[1 + core, second], halo.at[5 + core, second], 6, 4, -2)
+    far_down = far(halo.at[1 + core], halo.at[7 + core], 4, 2, -3)
+    far_up_own = far(own_ref, halo.at[0], 5, 3, 2)
+    lowest, highest = low == 0, low == depth - 1
+    helps_down, serves_down = low == 1, low == 2
+    serves_up = (low == depth - 2) & (core == 1)
     hands_down, hands_up = low != 0, (low != depth - 1) & (core == 1)
     outer = (pair == 0) | (pair == pairs - 1)
     inner = jnp.logical_not(outer)
@@ -256,18 +262,22 @@
                 own_ref[:, lanes].astype(jnp.float32) * factor
             ).astype(jnp.bfloat16)
     keep(0, stops[0], product(own_ref[...]))
-    pl.semaphore_wait(barrier, 5 + pairs - 1)
-    down.start()
+    pl.semaphore_wait(barrier, 7 + pairs - 1)
+    pl.when(lowest)(down_first.start)
+    pl.when(jnp.logical_not(lowest))(down.start)
     up.start()
     beside.start()
-
-    pl.when(serves_down)(far_down_own.start)
-
     pl.when(serves_up)(far_up_own.start)
     dispatch(0, stops[0])
     beside.wait_recv()
     tile(1, stops[1], halo[4 - core])
-    down.wait_recv()
+    pl.when(jnp.logical_not(highest))(down.wait_recv)
+
+    @pl.when(highest)
+    def _():
+        down_first.wait_recv()
+        down_second.wait_recv()
+
     down2 = link(halo.at[5 + core], 7 + core, 2, below)
 
     @pl.when(hands_down)
@@ -277,6 +287,8 @@
     cross_down = across(halo.at[5 + core], 5 + core, 1)
     cross_down.start()
     up.wait_recv()
+    pl.when(helps_down)(down_second.start)
+    pl.when(serves_down)(far_down.start)
     up2 = link(halo.at[2], 0, 3, above)
 
     @pl.when(hands_up)
@@ -314,10 +326,11 @@
     join(7)
     join(6)
 
-    for copy in (up, down, beside, cross_up, cross_down, last):
+    for copy in (up, beside, cross_up, cross_down, last):
         copy.wait_send()
     for taken, copy in (
-        (hands_down, down2), (hands_up, up2), (serves_down, far_down_own), (serves_up, far_up_own)
+        (lowest, down_first), (jnp.logical_not(lowest), down), (helps_down, down_second),
+        (hands_down, down2), (hands_up, up2), (serves_down, far_down), (serves_up, far_up_own)
     ):
         pl.when(taken)(copy.wait_send)
 
@@ -426,8 +439,8 @@
             pltpu.VMEM((4, 2, freqs * rows, rows), jnp.bfloat16),
             pltpu.VMEM((4, freqs * rows, rows), jnp.float32),
             pltpu.VMEM((4, freqs * rows, rows), jnp.bfloat16),
-            pltpu.SemaphoreType.DMA((6,)),
-            pltpu.SemaphoreType.DMA((4,)),
+            pltpu.SemaphoreType.DMA((7,)),
+            pltpu.SemaphoreType.DMA((5,)),
             pltpu.SemaphoreType.DMA((4,)),
             pltpu.SemaphoreType.DMA((4,)),
             pltpu.SemaphoreType.DMA((STEPS + 4,)),

time: 92.6 us -> 91 us (0.983)
  the two profiles are of different devices: /device:TPU:1 before, /device:TPU:128 now
where the time goes in v4:
time: 91 us; the launch traced here: 90.8 us
  Pallas kernels  85.5 us (94%)
  local copies, waits for them, and re-layouts  3.01 us (3%)
  matrix products  1.93 us (2%)
    pallas_call x1, Pallas kernels, shards(): pl.pallas_call(functools.partial(band_kernel, chips, depth), out_shape=ja...  53.5 us
    pallas_call x1, Pallas kernels, shards(): pl.pallas_call(functools.partial(route_kernel, chips, depth), out_shape=(...  32 us
    unnamed x11, local copies, waits for them, and re-layouts  2.1 us

profile of v4, /device:TPU:128, one launch (start us, length us, event | category | flops | bytes accessed | tf_op | source)
XLA Modules:
  0.0 90.8 jit_solution(14827655083714526631)
XLA Ops:
  0.0 0.0 copy-start
  0.0 0.0 copy-start.1
  0.0 0.7 copy-done.1
  0.7 0.2 convert_reduce_fusion
  0.9 0.1 copy-done
  1.1 1.1 %convolution_convert_fusion.2 = bf16[1024,128]{1,0:T(8,128)(2,1)S(1)} fusion(bf16[256,128]{1,0:T(8,128)(2,1)} %param.8, bf16[128,8,256]{2,1,0:T(8,128)(2,1)S(1)} %copy-done), kind=kOutput, calls=%fused_computation.2 | convolution fusion | flops 67239936 | bytes 851968 | tf_op jit(solution)/shard_map/dot_general | solution.py:380
  2.2 0.1 reshape.32
  2.3 0.3 convolution_convert_fusion
  2.6 0.2 reshape.33.out_ref
  2.8 32.0 %route.1 = (bf16[64,2,16,128]{3,2,1,0:T(8,128)(2,1)S(1)}, s32[8,8,2,1,128]{4,3,2,1,0:T(1,128)S(1)}) custom-call(s32[1,128]{1,0:T(1,128)S(1)} %bitcast.14, bf16[2,64,16,128]{3,2,1,0:T(8,128)(2,1)S(1)} %reshape.33.out_ref), custom_call_target="tpu_custom_call" | custom-call | tf_op jit(solution)/shard_map/route/pallas_call | solution.py:394
  34.9 0.1 copy.16
  35.0 0.2 select_reduce_fusion.1
  35.2 0.1 copy.20
  35.3 0.1 eq.72
  35.5 0.2 reshape.35
  35.7 0.0 copy-start.2
  35.7 0.0 copy-start.3
  35.7 0.0 copy-start.4
  35.8 0.3 convolution_convert_fusion.1.own_ref
  36.0 0.3 copy-done.2
  36.4 0.0 copy-done.3
  36.4 0.0 copy-done.4
  36.4 53.5 %band.1 = f32[6,128,256]{2,1,0:T(8,128)S(1)} custom-call(bf16[128,1024]{1,0:T(8,128)(2,1)S(1)} %convolution_convert_fusion.1.own_ref, f32[32]{0:T(128)S(1)} %copy-done.2, f32[1,128]{1,0:T(1,128)S(1)} %bitcast.15, s32[6]{0:T(128)S(1)} %copy-done.4), custom_call_target="tpu_custom_call" | custom-call | tf_op jit(solution)/shard_map/band/pallas_call | solution.py:429
  89.9 0.9 copy.22
  (4 shorter events, 0.0 us)
Async XLA Ops:
  0.0 1.1 %copy-start = (bf16[128,8,256]{2,1,0:T(8,128)(2,1)S(1)}, bf16[128,8,256]{2,1,0:T(8,128)(2,1)}, u32[]{:S(2)}) copy-start(bf16[128,8,256]{2,1,0:T(8,128)(2,1)} %param.6) | copy-start | bytes 1572868
  0.0 0.7 copy-start.1
  35.7 0.7 copy-start.2
  35.7 0.7 copy-start.3
  35.7 0.7 copy-start.4

commit v5 on v4

--- a/solution.py
+++ b/solution.py
@@ -153,7 +153,10 @@
     first, second = pl.ds(0, split), pl.ds(split, rows - split)
     down_first = far(own_ref.at[first], halo.at[5 + core, first], 1, 1, -1)
     down_second = far(halo.at[1 + core, second], halo.at[5 + core, second], 6, 4, -2)
-    far_down = far(halo.at[1 + core], halo.at[7 + core], 4, 2, -3)
+    share = rows // 4
+    near_rows, rest_rows = pl.ds(0, share), pl.ds(share, rows - share)
+    far_near = far(own_ref.at[near_rows], halo.at[7 + core, near_rows], 4, 2, -2)
+    far_rest = far(halo.at[1 + core, rest_rows], halo.at[7 + core, rest_rows], 4, 5, -3)
     far_up_own = far(own_ref, halo.at[0], 5, 3, 2)
     lowest, highest = low == 0, low == depth - 1
     helps_down, serves_down = low == 1, low == 2
@@ -267,6 +270,7 @@
     pl.when(jnp.logical_not(lowest))(down.start)
     up.start()
     beside.start()
+    pl.when(helps_down)(far_near.start)
     pl.when(serves_up)(far_up_own.start)
     dispatch(0, stops[0])
     beside.wait_recv()
@@ -288,7 +292,7 @@
     cross_down.start()
     up.wait_recv()
     pl.when(helps_down)(down_second.start)
-    pl.when(serves_down)(far_down.start)
+    pl.when(serves_down)(far_rest.start)
     up2 = link(halo.at[2], 0, 3, above)
 
     @pl.when(hands_up)
@@ -304,7 +308,13 @@
     cross_down.wait_recv()
     tiles((5, 4), (halo[6 - core], halo[2 - core]))
     last = across(halo.at[7 - 7 * core], 7 - 7 * core, 3)
-    down2.wait_recv()
+    pl.when(jnp.logical_not(highest))(down2.wait_recv)
+
+    @pl.when(highest)
+    def _():
+        far_near.wait_recv()
+        far_rest.wait_recv()
+
 
     @pl.when(core == 0)
     def _():
@@ -330,7 +340,7 @@
         copy.wait_send()
     for taken, copy in (
         (lowest, down_first), (jnp.logical_not(lowest), down), (helps_down, down_second),
-        (hands_down, down2), (hands_up, up2), (serves_down, far_down), (serves_up, far_up_own)
+        (hands_down, down2), (hands_up, up2), (helps_down, far_near), (serves_down, far_rest), (serves_up, far_up_own)
     ):
         pl.when(taken)(copy.wait_send)
 
@@ -440,7 +450,7 @@
             pltpu.VMEM((4, freqs * rows, rows), jnp.float32),
             pltpu.VMEM((4, freqs * rows, rows), jnp.bfloat16),
             pltpu.SemaphoreType.DMA((7,)),
-            pltpu.SemaphoreType.DMA((5,)),
+            pltpu.SemaphoreType.DMA((6,)),
             pltpu.SemaphoreType.DMA((4,)),
             pltpu.SemaphoreType.DMA((4,)),
             pltpu.SemaphoreType.DMA((STEPS + 4,)),

time: 91 us -> 88.6 us (0.974)
  the two profiles are of different devices: /device:TPU:128 before, /device:TPU:1 now
where the time goes in v5:
time: 88.6 us; the launch traced here: 87.5 us
  Pallas kernels  82.2 us (93%)
  local copies, waits for them, and re-layouts  3.01 us (3%)
  matrix products  1.92 us (2%)
    pallas_call x1, Pallas kernels, shards(): pl.pallas_call(functools.partial(band_kernel, chips, depth), out_shape=ja...  47.3 us
    pallas_call x1, Pallas kernels, shards(): pl.pallas_call(functools.partial(route_kernel, chips, depth), out_shape=(...  34.9 us
    unnamed x11, local copies, waits for them, and re-layouts  2.1 us

profile of v5, /device:TPU:1, one launch (start us, length us, event | category | flops | bytes accessed | tf_op | source)
XLA Modules:
  0.0 87.5 jit_solution(14360438056808844652)
XLA Ops:
  0.0 0.0 copy-start
  0.0 0.0 copy-start.1
  0.0 0.7 copy-done.1
  0.7 0.2 convert_reduce_fusion
  0.9 0.1 copy-done
  1.1 1.1 %convolution_convert_fusion.2 = bf16[1024,128]{1,0:T(8,128)(2,1)S(1)} fusion(bf16[256,128]{1,0:T(8,128)(2,1)} %param.8, bf16[128,8,256]{2,1,0:T(8,128)(2,1)S(1)} %copy-done), kind=kOutput, calls=%fused_computation.2 | convolution fusion | flops 67239936 | bytes 851968 | tf_op jit(solution)/shard_map/dot_general | solution.py:390
  2.2 0.1 reshape.32
  2.3 0.3 convolution_convert_fusion
  2.6 0.2 reshape.33.out_ref
  2.8 34.9 %route.1 = (bf16[64,2,16,128]{3,2,1,0:T(8,128)(2,1)S(1)}, s32[8,8,2,1,128]{4,3,2,1,0:T(1,128)S(1)}) custom-call(s32[1,128]{1,0:T(1,128)S(1)} %bitcast.14, bf16[2,64,16,128]{3,2,1,0:T(8,128)(2,1)S(1)} %reshape.33.out_ref), custom_call_target="tpu_custom_call" | custom-call | tf_op jit(solution)/shard_map/route/pallas_call | solution.py:404
  37.8 0.1 copy.16
  37.9 0.2 select_reduce_fusion.1
  38.1 0.1 copy.20
  38.2 0.1 eq.72
  38.4 0.2 reshape.35
  38.6 0.0 copy-start.2
  38.6 0.0 copy-start.3
  38.6 0.0 copy-start.4
  38.7 0.3 convolution_convert_fusion.1.own_ref
  38.9 0.3 copy-done.2
  39.3 0.0 copy-done.3
  39.3 0.0 copy-done.4
  39.3 47.3 %band.1 = f32[6,128,256]{2,1,0:T(8,128)S(1)} custom-call(bf16[128,1024]{1,0:T(8,128)(2,1)S(1)} %convolution_convert_fusion.1.own_ref, f32[32]{0:T(128)S(1)} %copy-done.2, f32[1,128]{1,0:T(1,128)S(1)} %bitcast.15, s32[6]{0:T(128)S(1)} %copy-done.4), custom_call_target="tpu_custom_call" | custom-call | tf_op jit(solution)/shard_map/band/pallas_call | solution.py:439
  86.6 0.9 %copy.22 = f32[6,128,256]{2,1,0:T(8,128)} copy(f32[6,128,256]{2,1,0:T(8,128)S(1)} %band.1) | data formatting | bytes 1572864
  (4 shorter events, 0.0 us)
Async XLA Ops:
  0.0 1.1 %copy-start = (bf16[128,8,256]{2,1,0:T(8,128)(2,1)S(1)}, bf16[128,8,256]{2,1,0:T(8,128)(2,1)}, u32[]{:S(2)}) copy-start(bf16[128,8,256]{2,1,0:T(8,128)(2,1)} %param.6) | copy-start | bytes 1572868
  0.0 0.7 copy-start.1
  38.6 0.7 copy-start.2
  38.6 0.7 copy-start.3
  38.6 0.7 copy-start.4

commit v6 on v5

--- a/solution.py
+++ b/solution.py
@@ -32,9 +32,10 @@
         return carry
 
     lax.fori_loop(1, chips, greet, 0)
+    ids[upper, low, core] = ids_ref[...]
+    staged[:, core] = out_ref[core]
     pl.semaphore_wait(barrier, chips)
 
-    ids[upper, low, core] = ids_ref[...]
     swap_ids = pltpu.make_async_remote_copy(
         ids.at[upper, low, core],
         ids.at[upper, low, core],
@@ -53,7 +54,6 @@
         device_id_type=MESH,
     )
     swap.start()
-    staged[:, core] = out_ref[core]
     swap_ids.wait()
     for i in range(1, depth):
         pltpu.make_async_remote_copy(
@@ -347,9 +347,10 @@
     scaling = 1.0 / 64.0
 
     def collect(hops):
-        for i in hops:
-            other = lax.rem(pair + i, pairs)
-            for half in range(2):
+        for half in (1, 0):
+            total = partial[half]
+            for i in hops:
+                other = lax.rem(pair + i, pairs)
                 pltpu.make_async_remote_copy(
                     outbox.at[0],
                     inbox.at[other, half],
@@ -358,8 +359,6 @@
                     device_id=(blk, other),
                     device_id_type=MESH,
                 ).wait_recv()
-        for half in range(2):
-            total = partial[half]
             for i in hops:
                 total = total + inbox[lax.rem(pair + i, pairs), half].astype(jnp.float32)
             result_ref[:, :, half * rows : (half + 1) * rows] = (total * scaling).reshape(freqs, rows, rows)

time: 88.6 us -> 88.5 us (level)
  no operation moved by 1% of the time
where the time goes in v6:
time: 88.5 us; the launch traced here: 87.5 us
  Pallas kernels  82.2 us (93%)
  local copies, waits for them, and re-layouts  3.01 us (3%)
  matrix products  1.91 us (2%)
    pallas_call x1, Pallas kernels, shards(): pl.pallas_call(functools.partial(band_kernel, chips, depth), out_shape=ja...  47.2 us
    pallas_call x1, Pallas kernels, shards(): pl.pallas_call(functools.partial(route_kernel, chips, depth), out_shape=(...  35 us
    unnamed x11, local copies, waits for them, and re-layouts  2.1 us

profile of v6, /device:TPU:1, one launch (start us, length us, event | category | flops | bytes accessed | tf_op | source)
XLA Modules:
  0.0 87.5 jit_solution(14821320395818446769)
XLA Ops:
  0.0 0.0 copy-start
  0.0 0.0 copy-start.1
  0.0 0.7 copy-done.1
  0.7 0.2 convert_reduce_fusion
  0.9 0.1 copy-done
  1.1 1.1 %convolution_convert_fusion.2 = bf16[1024,128]{1,0:T(8,128)(2,1)S(1)} fusion(bf16[256,128]{1,0:T(8,128)(2,1)} %param.8, bf16[128,8,256]{2,1,0:T(8,128)(2,1)S(1)} %copy-done), kind=kOutput, calls=%fused_computation.2 | convolution fusion | flops 67239936 | bytes 851968 | tf_op jit(solution)/shard_map/dot_general | solution.py:389
  2.2 0.1 reshape.32
  2.3 0.3 convolution_convert_fusion
  2.6 0.2 reshape.33.out_ref
  2.8 35.0 %route.1 = (bf16[64,2,16,128]{3,2,1,0:T(8,128)(2,1)S(1)}, s32[8,8,2,1,128]{4,3,2,1,0:T(1,128)S(1)}) custom-call(s32[1,128]{1,0:T(1,128)S(1)} %bitcast.14, bf16[2,64,16,128]{3,2,1,0:T(8,128)(2,1)S(1)} %reshape.33.out_ref), custom_call_target="tpu_custom_call" | custom-call | tf_op jit(solution)/shard_map/route/pallas_call | solution.py:403
  37.8 0.1 copy.16
  37.9 0.2 select_reduce_fusion.1
  38.2 0.1 copy.20
  38.3 0.1 eq.72
  38.4 0.2 reshape.35
  38.6 0.0 copy-start.2
  38.7 0.0 copy-start.3
  38.7 0.0 copy-start.4
  38.7 0.3 convolution_convert_fusion.1.own_ref
  39.0 0.3 copy-done.2
  39.3 0.0 copy-done.3
  39.3 0.0 copy-done.4
  39.3 47.2 %band.1 = f32[6,128,256]{2,1,0:T(8,128)S(1)} custom-call(bf16[128,1024]{1,0:T(8,128)(2,1)S(1)} %convolution_convert_fusion.1.own_ref, f32[32]{0:T(128)S(1)} %copy-done.2, f32[1,128]{1,0:T(1,128)S(1)} %bitcast.15, s32[6]{0:T(128)S(1)} %copy-done.4), custom_call_target="tpu_custom_call" | custom-call | tf_op jit(solution)/shard_map/band/pallas_call | solution.py:438
  86.6 0.9 %copy.22 = f32[6,128,256]{2,1,0:T(8,128)} copy(f32[6,128,256]{2,1,0:T(8,128)S(1)} %band.1) | data formatting | bytes 1572864
  (4 shorter events, 0.0 us)
Async XLA Ops:
  0.0 1.1 %copy-start = (bf16[128,8,256]{2,1,0:T(8,128)(2,1)S(1)}, bf16[128,8,256]{2,1,0:T(8,128)(2,1)}, u32[]{:S(2)}) copy-start(bf16[128,8,256]{2,1,0:T(8,128)(2,1)} %param.6) | copy-start | bytes 1572868
  0.0 0.7 copy-start.1
  38.6 0.7 copy-start.2
  38.7 0.7 copy-start.3
  38.7 0.7 copy-start.4
